TPU v7x, 256 devices: a whole 4x4x8 slice. The times are simulated.
256 devices in a mesh: row: 16 (over y_hi, z), col: 16 (over x, y_lo, core).
Axes of the slice: x: 4, y: 4 (y_hi: 2, y_lo: 2; y = y_hi * 2 + y_lo), z: 8, core: 2. Of those that a mesh axis runs over, the one named last changes fastest.
Arguments:
- inputs: bfloat16 [2048, 6144], P('col', 'row'), may hold values from -6 to 6
- out_grad: bfloat16 [2048, 6144], P('col', 'row'), may hold values from -6 to 6
- preact: bfloat16 [2048, 24576], P('row', 'col'), may hold values from -6 to 6
- w_in: bfloat16 [6144, 24576], P('row', 'col'), may hold values from -0.078125 to 0.078125
- w_out: bfloat16 [24576, 6144], P('col', 'row'), may hold values from -0.0390625 to 0.0390625
Outputs:
- input_grad: bfloat16 [2048, 6144], P('col', 'row')
- w_in_grad: float32 [6144, 24576], P('row', 'col')
- w_out_grad: float32 [24576, 6144], P('col', 'row')
All inputs are finite; a program needn't handle non-finite values.
Results may differ from a plain program's by a relative error of at most 0.005.
Values may be sent and summed in bfloat16 or wider, within the bound.
No kernel may reach another device: no remote copies, remote signals or barrier semaphores. Data moves between devices by JAX's collectives and lax.ppermute only.
A program may use at most 128 MiB of HBM per device.

v0:
```python
import jax
import jax.numpy as jnp
from jax import lax
from jax.sharding import PartitionSpec as P


def gelu_value(z):
    inner = 0.7978845608 * (z + 0.044715 * z * z * z)
    return 0.5 * z * (1.0 + jnp.tanh(inner))


def gelu_slope(z):
    inner = 0.7978845608 * (z + 0.044715 * z * z * z)
    tangent = jnp.tanh(inner)
    return 0.5 * (1.0 + tangent) + 0.5 * z * (1.0 - tangent * tangent) * 0.7978845608 * (
        1.0 + 3.0 * 0.044715 * z * z
    )


def local(inputs, out_grad, preact, w_in, w_out):
    grad_panel, input_panel = (
        lax.all_gather(out_grad, "col", axis=0, tiled=True),
        lax.all_gather(inputs, "col", axis=0, tiled=True),
    )
    preact_panel = lax.all_gather(preact, "row", axis=0, tiled=True)
    pre_float = preact_panel.astype(jnp.float32)
    hidden_panel = gelu_value(pre_float).astype(jnp.bfloat16)
    rows = grad_panel
    hidden_rows = lax.psum_scatter(
        lax.dot_general(rows, w_out, (((1,), (1,)), ((), ())), preferred_element_type=jnp.float32),
        "row",
        scatter_dimension=0,
        tiled=True,
    )
    local_grad = (hidden_rows * gelu_slope(preact.astype(jnp.float32))).astype(jnp.bfloat16)
    preact_grad_panel = lax.all_gather(local_grad, "row", axis=0, tiled=True)
    w_out_grad = lax.dot_general(
        hidden_panel, grad_panel, (((0,), (0,)), ((), ())), preferred_element_type=jnp.float32
    )
    w_in_grad = lax.dot_general(
        input_panel, preact_grad_panel, (((0,), (0,)), ((), ())), preferred_element_type=jnp.float32
    )
    rows = preact_grad_panel
    input_grad = lax.psum_scatter(
        lax.dot_general(rows, w_in, (((1,), (1,)), ((), ())), preferred_element_type=jnp.float32),
        "col",
        scatter_dimension=0,
        tiled=True,
    )
    return (input_grad.astype(jnp.bfloat16), w_in_grad, w_out_grad)


def solution(mesh):
    in_specs = (P("col", "row"), P("col", "row"), P("row", "col"), P("row", "col"), P("col", "row"))
    out_specs = (P("col", "row"), P("row", "col"), P("col", "row"))
    return jax.shard_map(local, mesh=mesh, in_specs=in_specs, out_specs=out_specs, check_vma=False)
```

profile of v0, /device:TPU:32, one launch (start us, length us, event | category | flops | bytes accessed | tf_op | source)
XLA Modules:
  0.0 654.0 jit_solution(13495451200928123844)
XLA Ops:
  7.2 0.0 all-gather.5.cloned.1.call-start
  7.2 0.7 all-gather.5.cloned.1.call-update
  7.9 0.0 reduce-scatter.3.cloned.1.call-start
  8.0 40.2 %all-gather.5.cloned.1.call-done = bf16[2048,384]{1,0:T(8,128)(2,1)} async-done(((bf16[128,384]{1,0:T(8,128)(2,1)}), bf16[2048,384]{1,0:T(8,128)(2,1)}) %all-gather.5.cloned.1.call-update) | async-done | bytes 1572880 | tf_op jit(solution)/shard_map/all_gather | solution.py:22
  48.1 7.9 %fusion.20 = f32[2048,1536]{1,0:T(8,128)} fusion(bf16[2048,384]{1,0:T(8,128)(2,1)} %all-gather.5.cloned.1.call-done, bf16[1536,384]{1,0:T(8,128)(2,1)S(1)} %copy-done), kind=kOutput, calls=%fused_computation.32 | convolution fusion | flops 2415919104 | bytes 15335424 | tf_op jit(solution)/shard_map/dot_general | solution.py:30
  56.0 0.0 reduce-scatter.3.cloned.1.call-update
  56.0 0.0 all-gather.7.cloned.1.call-start
  56.1 251.2 %reduce-scatter.3.cloned.1.call-done = f32[128,1536]{1,0:T(8,128)} async-done(((f32[2048,1536]{1,0:T(8,128)}), f32[128,1536]{1,0:T(8,128)}) %reduce-scatter.3.cloned.1.call-update) | async-done | bytes 786448 | tf_op jit(solution)/shard_map/reduce_scatter | solution.py:29
  307.2 2.4 fusion.14
  309.7 0.0 all-gather.7.cloned.1.call-update
  309.7 0.0 all-gather.11.cloned.1.call-start
  309.7 0.5 all-gather.11.cloned.1.call-update
  310.3 0.0 all-gather.9.cloned.1.call-start
  310.3 0.5 all-gather.9.cloned.1.call-update
  310.9 0.2 reduce-scatter.5.cloned.1.call-start
  311.1 113.5 %all-gather.7.cloned.1.call-done = bf16[2048,1536]{1,0:T(8,128)(2,1)} async-done(((bf16[128,1536]{1,0:T(8,128)(2,1)}), bf16[2048,1536]{1,0:T(8,128)(2,1)}) %all-gather.7.cloned.1.call-update) | async-done | bytes 6291472 | tf_op jit(solution)/shard_map/all_gather | solution.py:36
  424.5 8.2 %fusion.21 = f32[2048,384]{1,0:T(8,128)} fusion(bf16[2048,1536]{1,0:T(8,128)(2,1)} %all-gather.7.cloned.1.call-done, bf16[384,1536]{1,0:T(8,128)(2,1)} %param.8), kind=kOutput, calls=%fused_computation.33 | convolution fusion | flops 2415919104 | bytes 10616832 | tf_op jit(solution)/shard_map/dot_general | solution.py:45
  432.8 107.3 %all-gather.11.cloned.1.call-done = bf16[2048,1536]{1,0:T(8,128)(2,1)} async-done(((bf16[128,1536]{1,0:T(8,128)(2,1)}), bf16[2048,1536]{1,0:T(8,128)(2,1)}) %all-gather.11.cloned.1.call-update) | async-done | bytes 6291472 | tf_op jit(solution)/shard_map/all_gather | solution.py:25
  540.0 10.3 %fusion.5 = f32[1536,384]{1,0:T(8,128)} fusion(bf16[2048,384]{1,0:T(8,128)(2,1)S(1)} %copy-done.1, bf16[2048,1536]{1,0:T(8,128)(2,1)} %all-gather.11.cloned.1.call-done), kind=kOutput, calls=%fused_computation.10 | convolution fusion | flops 2447376384 | bytes 10223616 | tf_op jit(solution)/shard_map/dot_general | solution.py:37
  550.3 24.5 %all-gather.9.cloned.1.call-done = bf16[2048,384]{1,0:T(8,128)(2,1)} async-done(((bf16[128,384]{1,0:T(8,128)(2,1)}), bf16[2048,384]{1,0:T(8,128)(2,1)}) %all-gather.9.cloned.1.call-update) | async-done | bytes 1572880 | tf_op jit(solution)/shard_map/all_gather | solution.py:23
  574.8 6.0 convolution_bitcast_fusion
  580.8 2.0 copy.8
  582.7 62.8 %reduce-scatter.5.cloned.1.call-done = f32[128,384]{1,0:T(8,128)} async-done(((f32[2048,384]{1,0:T(8,128)}), f32[128,384]{1,0:T(8,128)}) %reduce-scatter.5.cloned.1.call-update) | async-done | bytes 196624 | tf_op jit(solution)/shard_map/reduce_scatter | solution.py:44
  645.6 1.6 convert_element_type.17
  (7 shorter events, 0.0 us)
Async XLA Ops:
  7.2 41.0 %copy-start = (bf16[1536,384]{1,0:T(8,128)(2,1)S(1)}, bf16[1536,384]{1,0:T(8,128)(2,1)}, u32[]{:S(2)}) copy-start(bf16[1536,384]{1,0:T(8,128)(2,1)} %param.9) | copy-start | bytes 3538948
  7.2 41.0 %all-gather.5.cloned.1.call-start = ((), (), s32[]{:S(2)}) async-start(), calls=%async_computation.2 | async-start | bytes 1671168 | tf_op jit(solution)/shard_map/all_gather | solution.py:22
  7.9 299.3 %reduce-scatter.3.cloned.1.call-start = ((), (), s32[]{:S(2)}) async-start(), calls=%async_computation.3 | async-start | bytes 13369344 | tf_op jit(solution)/shard_map/reduce_scatter | solution.py:29
  56.0 251.2 %copy-start.2 = (bf16[128,1536]{1,0:T(8,128)(2,1)S(1)}, bf16[128,1536]{1,0:T(8,128)(2,1)}, u32[]{:S(2)}) copy-start(bf16[128,1536]{1,0:T(8,128)(2,1)} %param.7) | copy-start | bytes 1179652
  56.0 368.5 %all-gather.7.cloned.1.call-start = ((), (), s32[]{:S(2)}) async-start(), calls=%async_computation.4 | async-start | bytes 6684672 | tf_op jit(solution)/shard_map/all_gather | solution.py:36
  309.7 230.4 %all-gather.11.cloned.1.call-start = ((), (), s32[]{:S(2)}) async-start(), calls=%async_computation.7 | async-start | bytes 6684672 | tf_op jit(solution)/shard_map/all_gather | solution.py:25
  310.3 264.5 %all-gather.9.cloned.1.call-start = ((), (), s32[]{:S(2)}) async-start(), calls=%async_computation.6 | async-start | bytes 1671168 | tf_op jit(solution)/shard_map/all_gather | solution.py:23
  310.8 229.2 %copy-start.1 = (bf16[2048,384]{1,0:T(8,128)(2,1)S(1)}, bf16[2048,384]{1,0:T(8,128)(2,1)}, u32[]{:S(2)}) copy-start(bf16[2048,384]{1,0:T(8,128)(2,1)} %all-gather.5.cloned.1.call-done) | copy-start | bytes 4718596
  310.9 334.7 %reduce-scatter.5.cloned.1.call-start = ((), (), s32[]{:S(2)}) async-start(), calls=%async_computation.5 | async-start | bytes 3342336 | tf_op jit(solution)/shard_map/reduce_scatter | solution.py:44
Sparse Core Ops, SparseCore 0:
  9.9 38.2 all-gather.4
  56.2 251.0 reduce-scatter.2
  310.8 113.7 all-gather.6
  427.3 112.6 all-gather.10
  541.9 32.8 all-gather.8
  577.4 68.1 reduce-scatter.4
where the time goes:
time: 654 us
  waiting for transfers between devices  601 us (92%)
  matrix products  32.3 us (5%)
  between operations  14.1 us (2%)
    reduce_scatter x1, waiting for transfers between devices, local(): lax.psum_scatter(lax.dot_general(rows, w_out, (((1,), (1,)), ((), ())), p...  251 us
    all_gather x1, waiting for transfers between devices, local(): preact_grad_panel = lax.all_gather(local_grad, 'row', axis=0, tiled=True)  113 us
    all_gather x1, waiting for transfers between devices, local(): preact_panel = lax.all_gather(preact, 'row', axis=0, tiled=True)  107 us
    reduce_scatter x1, waiting for transfers between devices, local(): lax.psum_scatter(lax.dot_general(rows, w_in, (((1,), (1,)), ((), ())), pr...  62.8 us
    all_gather x1, waiting for transfers between devices, local(): lax.all_gather(out_grad, 'col', axis=0, tiled=True)  40.2 us
    all_gather x1, waiting for transfers between devices, local(): lax.all_gather(inputs, 'col', axis=0, tiled=True)  24.5 us
  transfers between devices with their start and end apart: 6, of which 6 were waited for; matrix products, arithmetic and copies ran while one was open for 4% of the time, Pallas kernels for 0%

commit v1 on v0

--- a/solution.py
+++ b/solution.py
@@ -2,6 +2,11 @@
 import jax.numpy as jnp
 from jax import lax
 from jax.sharding import PartitionSpec as P
+
+
+def exchange_gather(value, axis, dim):
+    repeated = jnp.stack([value] * lax.axis_size(axis))
+    return jnp.concatenate(lax.all_to_all(repeated, axis, 0, 0), axis=dim)
 
 
 def gelu_value(z):
@@ -33,7 +38,7 @@
         tiled=True,
     )
     local_grad = (hidden_rows * gelu_slope(preact.astype(jnp.float32))).astype(jnp.bfloat16)
-    preact_grad_panel = lax.all_gather(local_grad, "row", axis=0, tiled=True)
+    preact_grad_panel = exchange_gather(local_grad, "row", 0)
     w_out_grad = lax.dot_general(
         hidden_panel, grad_panel, (((0,), (0,)), ((), ())), preferred_element_type=jnp.float32
     )

time: 654 us -> 632 us (0.966)
  waiting for transfers between devices: 601 us -> 570 us
    all_to_all x0 -> x1, waiting for transfers between devices: none -> 162 us  [exchange_gather(): return jnp.concatenate(lax.all_to_all(repeated, axis, 0, 0), axis=dim)]
    all_gather x1 -> x0, waiting for transfers between devices: 113 us -> none  [local(): preact_grad_panel = lax.all_gather(local_grad, 'row', axis=0, tiled=True)]
    all_gather x1, waiting for transfers between devices: 107 us -> 27.9 us  [local(): preact_panel = lax.all_gather(preact, 'row', axis=0, tiled=True)]
  transfers between devices with their start and end apart: 6 -> 6, of which waited for: 6 -> 6; matrix products, arithmetic and copies ran while one was open for 4% -> 5% of each run, Pallas kernels for 0% -> 0%
where the time goes in v1:
time: 632 us; the launch traced here: 631 us
  waiting for transfers between devices  570 us (90%)
  matrix products  32.6 us (5%)
  between operations  13.8 us (2%)
  starting transfers between devices  6.81 us (1%)
    reduce_scatter x1, waiting for transfers between devices, local(): lax.psum_scatter(lax.dot_general(rows, w_out, (((1,), (1,)), ((), ())), p...  250 us
    all_to_all x1, waiting for transfers between devices, exchange_gather(): return jnp.concatenate(lax.all_to_all(repeated, axis, 0, 0), axis=dim)  162 us
    reduce_scatter x1, waiting for transfers between devices, local(): lax.psum_scatter(lax.dot_general(rows, w_in, (((1,), (1,)), ((), ())), pr...  62.8 us
    all_gather x1, waiting for transfers between devices, local(): lax.all_gather(out_grad, 'col', axis=0, tiled=True)  40.2 us
    all_gather x1, waiting for transfers between devices, local(): preact_panel = lax.all_gather(preact, 'row', axis=0, tiled=True)  27.9 us
    all_gather x1, waiting for transfers between devices, local(): lax.all_gather(inputs, 'col', axis=0, tiled=True)  24.4 us
  transfers between devices with their start and end apart: 6, of which 6 were waited for; matrix products, arithmetic and copies ran while one was open for 5% of the time, Pallas kernels for 0%

profile of v1, /device:TPU:32, one launch (start us, length us, event | category | flops | bytes accessed | tf_op | source)
XLA Modules:
  0.0 631.3 jit_solution(8090663042179594420)
XLA Ops:
  7.2 0.0 all-gather.4.cloned.1.call-start
  7.2 0.7 all-gather.4.cloned.1.call-update
  7.9 0.0 reduce-scatter.3.cloned.1.call-start
  8.0 40.2 %all-gather.4.cloned.1.call-done = bf16[2048,384]{1,0:T(8,128)(2,1)} async-done(((bf16[128,384]{1,0:T(8,128)(2,1)}), bf16[2048,384]{1,0:T(8,128)(2,1)}) %all-gather.4.cloned.1.call-update) | async-done | bytes 1572880 | tf_op jit(solution)/shard_map/all_gather | solution.py:27
  48.1 7.9 %fusion.20 = f32[2048,1536]{1,0:T(8,128)} fusion(bf16[2048,384]{1,0:T(8,128)(2,1)} %all-gather.4.cloned.1.call-done, bf16[1536,384]{1,0:T(8,128)(2,1)S(1)} %copy-done), kind=kOutput, calls=%fused_computation.32 | convolution fusion | flops 2415919104 | bytes 15335424 | tf_op jit(solution)/shard_map/dot_general | solution.py:35
  56.0 0.0 reduce-scatter.3.cloned.1.call-update
  56.0 0.0 all-gather.8.cloned.1.call-start
  56.1 0.7 all-gather.8.cloned.1.call-update
  56.8 250.5 %reduce-scatter.3.cloned.1.call-done = f32[128,1536]{1,0:T(8,128)} async-done(((f32[2048,1536]{1,0:T(8,128)}), f32[128,1536]{1,0:T(8,128)}) %reduce-scatter.3.cloned.1.call-update) | async-done | bytes 786448 | tf_op jit(solution)/shard_map/reduce_scatter | solution.py:34
  307.2 1.7 fusion.14
  308.9 3.3 stack.2
  312.1 6.4 %all-to-all-start = ((bf16[16,128,1536]{2,1,0:T(8,128)(2,1)}), bf16[16,128,1536]{2,1,0:T(8,128)(2,1)}, u32[]{:S(2)}, u32[]{:S(2)}) async-start(bf16[16,128,1536]{2,1,0:T(8,128)(2,1)} %stack.2), calls=%async_computation.1 | async-start | bytes 12582912 | tf_op jit(solution)/shard_map/all_to_all | solution.py:9
  318.6 0.0 all-gather.6.cloned.1.call-start
  318.6 0.5 all-gather.6.cloned.1.call-update
  319.2 0.2 reduce-scatter.5.cloned.1.call-start
  319.4 162.0 %all-to-all-done = bf16[16,128,1536]{2,1,0:T(8,128)(2,1)} async-done(((bf16[16,128,1536]{2,1,0:T(8,128)(2,1)}), bf16[16,128,1536]{2,1,0:T(8,128)(2,1)}, u32[]{:S(2)}, u32[]{:S(2)}) %all-to-all-start) | async-done | bytes 6291488 | tf_op jit(solution)/shard_map/all_to_all | solution.py:9
  481.4 8.4 %fusion.21 = f32[2048,384]{1,0:T(8,128)} fusion(bf16[2048,1536]{1,0:T(8,128)(2,1)} %bitcast, bf16[384,1536]{1,0:T(8,128)(2,1)} %param.8), kind=kOutput, calls=%fused_computation.33 | convolution fusion | flops 2415919104 | bytes 10616832 | tf_op jit(solution)/shard_map/dot_general | solution.py:50
  489.9 27.9 %all-gather.8.cloned.1.call-done = bf16[2048,1536]{1,0:T(8,128)(2,1)} async-done(((bf16[128,1536]{1,0:T(8,128)(2,1)}), bf16[2048,1536]{1,0:T(8,128)(2,1)}) %all-gather.8.cloned.1.call-update) | async-done | bytes 6291472 | tf_op jit(solution)/shard_map/all_gather | solution.py:30
  517.8 10.3 %fusion.5 = f32[1536,384]{1,0:T(8,128)} fusion(bf16[2048,384]{1,0:T(8,128)(2,1)S(1)} %copy-done.1, bf16[2048,1536]{1,0:T(8,128)(2,1)} %all-gather.8.cloned.1.call-done), kind=kOutput, calls=%fused_computation.10 | convolution fusion | flops 2447376384 | bytes 10223616 | tf_op jit(solution)/shard_map/dot_general | solution.py:42
  528.1 24.4 %all-gather.6.cloned.1.call-done = bf16[2048,384]{1,0:T(8,128)(2,1)} async-done(((bf16[128,384]{1,0:T(8,128)(2,1)}), bf16[2048,384]{1,0:T(8,128)(2,1)}) %all-gather.6.cloned.1.call-update) | async-done | bytes 1572880 | tf_op jit(solution)/shard_map/all_gather | solution.py:28
  552.5 6.0 convolution_bitcast_fusion
  558.5 2.0 copy.8
  560.4 62.8 %reduce-scatter.5.cloned.1.call-done = f32[128,384]{1,0:T(8,128)} async-done(((f32[2048,384]{1,0:T(8,128)}), f32[128,384]{1,0:T(8,128)}) %reduce-scatter.5.cloned.1.call-update) | async-done | bytes 196624 | tf_op jit(solution)/shard_map/reduce_scatter | solution.py:49
  623.2 1.6 convert_element_type.17
  (7 shorter events, 0.0 us)
Async XLA Ops:
  7.2 41.0 %copy-start = (bf16[1536,384]{1,0:T(8,128)(2,1)S(1)}, bf16[1536,384]{1,0:T(8,128)(2,1)}, u32[]{:S(2)}) copy-start(bf16[1536,384]{1,0:T(8,128)(2,1)} %param.9) | copy-start | bytes 3538948
  7.2 41.0 %all-gather.4.cloned.1.call-start = ((), (), s32[]{:S(2)}) async-start(), calls=%async_computation.3 | async-start | bytes 1671168 | tf_op jit(solution)/shard_map/all_gather | solution.py:27
  7.9 299.3 %reduce-scatter.3.cloned.1.call-start = ((), (), s32[]{:S(2)}) async-start(), calls=%async_computation.4 | async-start | bytes 13369344 | tf_op jit(solution)/shard_map/reduce_scatter | solution.py:34
  56.0 251.2 %copy-start.2 = (bf16[128,1536]{1,0:T(8,128)(2,1)S(1)}, bf16[128,1536]{1,0:T(8,128)(2,1)}, u32[]{:S(2)}) copy-start(bf16[128,1536]{1,0:T(8,128)(2,1)} %param.7) | copy-start | bytes 1179652
  56.0 461.8 %all-gather.8.cloned.1.call-start = ((), (), s32[]{:S(2)}) async-start(), calls=%async_computation.7 | async-start | bytes 6684672 | tf_op jit(solution)/shard_map/all_gather | solution.py:30
  312.1 169.3 %all-to-all-start = ((bf16[16,128,1536]{2,1,0:T(8,128)(2,1)}), bf16[16,128,1536]{2,1,0:T(8,128)(2,1)}, u32[]{:S(2)}, u32[]{:S(2)}) async-start(bf16[16,128,1536]{2,1,0:T(8,128)(2,1)} %stack.2), calls=%async_computation.1 | async-start | bytes 12582912 | tf_op jit(solution)/shard_map/all_to_all | solution.py:9
  318.6 233.9 %all-gather.6.cloned.1.call-start = ((), (), s32[]{:S(2)}) async-start(), calls=%async_computation.6 | async-start | bytes 1671168 | tf_op jit(solution)/shard_map/all_gather | solution.py:28
  319.2 304.1 %reduce-scatter.5.cloned.1.call-start = ((), (), s32[]{:S(2)}) async-start(), calls=%async_computation.5 | async-start | bytes 3342336 | tf_op jit(solution)/shard_map/reduce_scatter | solution.py:49
  481.4 36.4 %copy-start.1 = (bf16[2048,384]{1,0:T(8,128)(2,1)S(1)}, bf16[2048,384]{1,0:T(8,128)(2,1)}, u32[]{:S(2)}) copy-start(bf16[2048,384]{1,0:T(8,128)(2,1)} %all-gather.4.cloned.1.call-done) | copy-start | bytes 4718596
Sparse Core Ops, SparseCore 0:
  9.9 38.2 all-gather.3
  56.1 251.0 reduce-scatter.2
  310.2 207.6 all-gather.7
  519.7 32.7 all-gather.5
  555.0 68.1 reduce-scatter.4
